TPU v7x, 256 devices: a whole 4x4x8 slice. The times are simulated.
256 devices in a mesh: src: 8 (over z_hi, y), tgt: 32 (over z_lo, x, core).
Axes of the slice: x: 4, y: 4, z: 8 (z_hi: 2, z_lo: 4; z = z_hi * 4 + z_lo), core: 2. Of those that a mesh axis runs over, the one named last changes fastest.
Arguments:
- source_points: bfloat16 [16384, 128], P(('src', 'tgt')), may hold values from -1 to 1
- target_points: bfloat16 [32768, 128], P(('tgt', 'src')), may hold values from -1 to 1
- source_mass: float32 [16384], P('src'), may hold values from 0.1 to 10
- target_mass: float32 [32768], P('tgt'), may hold values from 0.1 to 10
Outputs:
- source_potential: float32 [16384], P('src')
- target_potential: float32 [32768], P('tgt')
All inputs are finite; a program needn't handle non-finite values.
Results may differ from a plain program's by a relative error of at most 0.0003.
Values may be sent and summed in bfloat16 or wider, within the bound.
A program may use at most 64 MiB of HBM per device.

v0:
```python
import math

import jax
import jax.numpy as jnp
from jax import lax
from jax.sharding import PartitionSpec as P

ITERS = 3


EPS = 0.05


def half_norm(points):
    values = points.astype(jnp.float32)
    return 0.5 * jnp.sum(values * values, axis=1)


def tile_cost(rows, rows_half, cols, cols_half):
    return (
        rows_half[:, None]
        + cols_half[None, :]
        - jnp.dot(rows, cols.T, preferred_element_type=jnp.float32)
    )


def combine(first, second):
    peak = jnp.maximum(first[0], second[0])
    return (peak, first[1] * jnp.exp(first[0] - peak) + second[1] * jnp.exp(second[0] - peak))


def finish_rows(peak, total):
    widest = lax.pmax(peak, "tgt")
    total = lax.psum(total * jnp.exp(peak - widest), "tgt")
    peak = widest
    return -EPS * (peak + jnp.log(total))


def finish_cols(peak, total):
    widest = lax.pmax(peak, "src")
    total = lax.psum(total * jnp.exp(peak - widest), "src")
    peak = widest
    return -EPS * (peak + jnp.log(total))


def row_stats(scores):
    peak = jnp.max(scores, axis=1)
    return (peak, jnp.sum(jnp.exp(scores - peak[:, None]), axis=1))


def col_stats(scores):
    peak = jnp.max(scores, axis=0)
    return (peak, jnp.sum(jnp.exp(scores - peak[None, :]), axis=0))


def local(source_points, target_points, source_mass, target_mass):
    sources = lax.all_gather(source_points, "tgt", axis=0, tiled=True)
    targets = lax.all_gather(target_points, "src", axis=0, tiled=True)
    source_half = half_norm(sources)
    target_half = half_norm(targets)
    log_a = jnp.log(source_mass)
    log_b = jnp.log(target_mass)
    count = sources.shape[0]
    width = targets.shape[0]
    block = math.gcd(512, count)
    steps_count = count // block
    source_blocks = sources.reshape(steps_count, block, sources.shape[1])
    half_blocks = source_half.reshape(steps_count, block)
    target_potential = jnp.zeros((width,), jnp.float32)
    source_potential = jnp.zeros((count,), jnp.float32)
    for step in range(ITERS):
        shift_cols = target_potential + EPS * log_b

        def block_rows(pair):
            chosen, chosen_half = pair
            cost = tile_cost(chosen, chosen_half, targets, target_half)
            return row_stats((shift_cols[None, :] - cost) / EPS)

        peak, total = lax.map(block_rows, (source_blocks, half_blocks))
        peak = peak.reshape(count)
        total = total.reshape(count)
        source_potential = finish_rows(peak, total)
        shift_rows = source_potential + EPS * log_a
        shift_blocks = shift_rows.reshape(steps_count, block)

        def block_cols(carry, pieces):
            chosen, chosen_half, chosen_shift = pieces
            cost = tile_cost(chosen, chosen_half, targets, target_half)
            return (combine(carry, col_stats((chosen_shift[:, None] - cost) / EPS)), None)

        start = (jnp.full((width,), -1e30, jnp.float32), jnp.zeros((width,), jnp.float32))
        (peak, total), unused = lax.scan(
            block_cols, start, (source_blocks, half_blocks, shift_blocks)
        )
        target_potential = finish_cols(peak, total)
    return (source_potential, target_potential)


def solution(mesh):
    placed = (P(("src", "tgt"), None), P(("tgt", "src"), None), P("src"), P("tgt"))
    return jax.shard_map(
        local, mesh=mesh, in_specs=placed, out_specs=(P("src"), P("tgt")), check_vma=False
    )
```

profile of v0, /device:TPU:1, one launch (start us, length us, event | category | flops | bytes accessed | tf_op | source)
XLA Modules:
  0.0 677.8 jit_solution(18199802177442221580)
XLA Ops:
  0.6 41.1 %all_gather.7 = bf16[1024,128]{1,0:T(8,128)(2,1)S(1)} all-gather(bf16[128,128]{1,0:T(8,128)(2,1)} %param.17), channel_id=1, replica_groups=mesh['src'=8,'tgt'=32] {'src'}, dimensions={0}, use_global_device_ids=true | all-gather | bytes 294912 | tf_op jit(solution)/shard_map/all_gather | solution.py:58
  42.0 50.5 %all_gather.6 = bf16[2048,128]{1,0:T(8,128)(2,1)S(1)} all-gather(bf16[64,128]{1,0:T(8,128)(2,1)} %param.16), channel_id=1, replica_groups=mesh['src'=8,'tgt'=32] {'tgt'}, dimensions={0}, use_global_device_ids=true | all-gather | bytes 540672 | tf_op jit(solution)/shard_map/all_gather | solution.py:57
  92.5 0.3 multiply_reduce_fusion
  92.8 0.7 log_multiply_fusion.1
  93.6 5.0 while.75
  93.6 0.6 fusion.50
  94.2 0.5 exponential_reduce_fusion.12
  94.8 0.6 fusion.50
  95.4 0.5 exponential_reduce_fusion.12
  96.1 0.6 fusion.50
  96.7 0.5 exponential_reduce_fusion.12
  97.3 0.6 fusion.50
  97.9 0.5 exponential_reduce_fusion.12
  98.5 67.9 %pmax.42 = f32[2048]{0:T(1024)S(1)} all-reduce(f32[2048]{0:T(1024)S(1)} %bitcast.125), channel_id=1, replica_groups=mesh['src'=8,'tgt'=32] {'tgt'}, use_global_device_ids=true, to_apply=%region_6.7 | all-reduce | flops 2048 | bytes 16384 | tf_op jit(solution)/shard_map/pmax | solution.py:33
  166.4 68.8 %psum.42 = f32[2048]{0:T(1024)S(1)} all-reduce(f32[2048]{0:T(1024)S(1)} %exponential_multiply_fusion.2), channel_id=1, replica_groups=mesh['src'=8,'tgt'=32] {'tgt'}, use_global_device_ids=true, to_apply=%region_7.8 | all-reduce | flops 2048 | bytes 16384 | tf_op jit(solution)/shard_map/psum | solution.py:34
  235.3 3.7 while.78
  235.3 0.5 fusion.56
  236.2 0.5 fusion.56
  236.8 0.3 exponential_reduce_fusion.15
  237.2 0.5 fusion.56
  237.7 0.3 exponential_reduce_fusion.15
  238.1 0.5 fusion.56
  239.0 26.9 %pmax.43 = f32[1024]{0:T(1024)S(1)} all-reduce(f32[1024]{0:T(1024)S(1)} %get-tuple-element.262), channel_id=1, replica_groups=mesh['src'=8,'tgt'=32] {'src'}, use_global_device_ids=true, to_apply=%region_12.13 | all-reduce | flops 1024 | bytes 8192 | tf_op jit(solution)/shard_map/pmax | solution.py:40
  265.9 20.3 %psum.43 = f32[1024]{0:T(1024)S(1)} all-reduce(f32[1024]{0:T(1024)S(1)} %exponential_multiply_fusion.5), channel_id=1, replica_groups=mesh['src'=8,'tgt'=32] {'src'}, use_global_device_ids=true, to_apply=%region_13.14 | all-reduce | flops 1024 | bytes 8192 | tf_op jit(solution)/shard_map/psum | solution.py:41
  286.3 5.0 while.76
  286.3 0.6 fusion.52
  286.9 0.5 exponential_reduce_fusion.13
  287.5 0.6 fusion.52
  288.1 0.5 exponential_reduce_fusion.13
  288.8 0.6 fusion.52
  289.4 0.5 exponential_reduce_fusion.13
  290.0 0.6 fusion.52
  290.6 0.5 exponential_reduce_fusion.13
  291.2 75.6 %pmax.44 = f32[2048]{0:T(1024)S(1)} all-reduce(f32[2048]{0:T(1024)S(1)} %bitcast.127), channel_id=1, replica_groups=mesh['src'=8,'tgt'=32] {'tgt'}, use_global_device_ids=true, to_apply=%region_18.19 | all-reduce | flops 2048 | bytes 16384 | tf_op jit(solution)/shard_map/pmax | solution.py:33
  366.9 68.4 %psum.44 = f32[2048]{0:T(1024)S(1)} all-reduce(f32[2048]{0:T(1024)S(1)} %exponential_multiply_fusion.1), channel_id=1, replica_groups=mesh['src'=8,'tgt'=32] {'tgt'}, use_global_device_ids=true, to_apply=%region_19.20 | all-reduce | flops 2048 | bytes 16384 | tf_op jit(solution)/shard_map/psum | solution.py:34
  435.4 3.7 while.79
  435.4 0.5 fusion.59
  436.3 0.5 fusion.59
  437.3 0.5 fusion.59
  437.8 0.3 exponential_reduce_fusion.16
  438.2 0.5 fusion.59
  438.7 0.3 exponential_reduce_fusion.16
  439.1 22.1 %pmax.45 = f32[1024]{0:T(1024)S(1)} all-reduce(f32[1024]{0:T(1024)S(1)} %get-tuple-element.266), channel_id=1, replica_groups=mesh['src'=8,'tgt'=32] {'src'}, use_global_device_ids=true, to_apply=%region_24.25 | all-reduce | flops 1024 | bytes 8192 | tf_op jit(solution)/shard_map/pmax | solution.py:40
  461.2 20.3 %psum.45 = f32[1024]{0:T(1024)S(1)} all-reduce(f32[1024]{0:T(1024)S(1)} %exponential_multiply_fusion.4), channel_id=1, replica_groups=mesh['src'=8,'tgt'=32] {'src'}, use_global_device_ids=true, to_apply=%region_25.26 | all-reduce | flops 1024 | bytes 8192 | tf_op jit(solution)/shard_map/psum | solution.py:41
  481.5 5.0 while.77
  481.5 0.6 fusion.54
  482.1 0.5 exponential_reduce_fusion.14
  482.8 0.6 fusion.54
  483.4 0.5 exponential_reduce_fusion.14
  484.0 0.6 fusion.54
  484.6 0.5 exponential_reduce_fusion.14
  485.3 0.6 fusion.54
  485.8 0.5 exponential_reduce_fusion.14
  486.5 75.6 %pmax.46 = f32[2048]{0:T(1024)S(1)} all-reduce(f32[2048]{0:T(1024)S(1)} %bitcast.129), channel_id=1, replica_groups=mesh['src'=8,'tgt'=32] {'tgt'}, use_global_device_ids=true, to_apply=%region_30.31 | all-reduce | flops 2048 | bytes 16384 | tf_op jit(solution)/shard_map/pmax | solution.py:33
  562.1 68.4 %psum.46 = f32[2048]{0:T(1024)S(1)} all-reduce(f32[2048]{0:T(1024)S(1)} %exponential_multiply_fusion), channel_id=1, replica_groups=mesh['src'=8,'tgt'=32] {'tgt'}, use_global_device_ids=true, to_apply=%region_31.32 | all-reduce | flops 2048 | bytes 16384 | tf_op jit(solution)/shard_map/psum | solution.py:34
  630.5 0.6 fusion.21
  631.1 3.7 while.80
  631.1 0.5 fusion.62
  632.1 0.5 fusion.62
  633.0 0.5 fusion.62
  633.9 0.5 fusion.62
  634.8 22.1 %pmax.47 = f32[1024]{0:T(1024)S(1)} all-reduce(f32[1024]{0:T(1024)S(1)} %get-tuple-element.270), channel_id=1, replica_groups=mesh['src'=8,'tgt'=32] {'src'}, use_global_device_ids=true, to_apply=%region_36.37 | all-reduce | flops 1024 | bytes 8192 | tf_op jit(solution)/shard_map/pmax | solution.py:40
  656.9 20.3 %psum.47 = f32[1024]{0:T(1024)S(1)} all-reduce(f32[1024]{0:T(1024)S(1)} %exponential_multiply_fusion.3), channel_id=1, replica_groups=mesh['src'=8,'tgt'=32] {'src'}, use_global_device_ids=true, to_apply=%region_37.38 | all-reduce | flops 1024 | bytes 8192 | tf_op jit(solution)/shard_map/psum | solution.py:41
  677.2 0.6 add_multiply_fusion.1
  (107 shorter events, 4.6 us)
Async XLA Ops:
  93.5 141.7 %copy-start = (f32[2048]{0:T(1024)S(1)}, f32[2048]{0:T(1024)}, u32[]{:S(2)}) copy-start(f32[2048]{0:T(1024)} %param.18) | copy-start | bytes 24580
  235.3 51.0 %copy-start.1 = (f32[1024]{0:T(1024)S(1)}, f32[1024]{0:T(1024)}, u32[]{:S(2)}) copy-start(f32[1024]{0:T(1024)} %param.19) | copy-start | bytes 12292
where the time goes:
time: 685 us; the launch traced here: 678 us
  blocking collectives  648 us (95%)
  matrix products  13.5 us (2%)
  other arithmetic  13 us (2%)
    pmax x3, blocking collectives, finish_rows(): widest = lax.pmax(peak, 'tgt')  219 us
    psum x3, blocking collectives, finish_rows(): total = lax.psum(total * jnp.exp(peak - widest), 'tgt')  206 us
    pmax x3, blocking collectives, finish_cols(): widest = lax.pmax(peak, 'src')  71.1 us
    psum x3, blocking collectives, finish_cols(): total = lax.psum(total * jnp.exp(peak - widest), 'src')  60.9 us
    all_gather x1, blocking collectives, local(): sources = lax.all_gather(source_points, 'tgt', axis=0, tiled=True)  50.5 us
    all_gather x1, blocking collectives, local(): targets = lax.all_gather(target_points, 'src', axis=0, tiled=True)  41.1 us

commit v1 on v0

v1 whole, which is shorter than its diff:
```python
import math

import jax
import jax.numpy as jnp
from jax import lax
from jax.experimental import pallas as pl
from jax.experimental.pallas import tpu as pltpu
from jax.sharding import PartitionSpec as P

MESH = pl.DeviceIdType.MESH

ITERS = 3
EPS = 0.05
ALPHA = 1.0 / (EPS * math.log(2.0))
INV_LN2 = 1.0 / math.log(2.0)

TILES = 16
CHUNKS = 8
HALVES = 2


def log2(value):
    return jnp.log(value) * INV_LN2


def place(z, y, x, c):
    return {"src": (z // 4) * 4 + y, "tgt": (z % 4) * 8 + x * 2 + c}


def chunk_of(z):
    return (z % 4) * 2 + z // 4


def plane_peer(p, z, y, x, c):
    return place(z, (y + p // 8) % 4, (x + (p // 2) % 4) % 4, (c + p % 2) % 2)


def row_norm(points):
    values = points.astype(jnp.float32)
    square = values * values
    high = square.astype(jnp.bfloat16)
    low = (square - high.astype(jnp.float32)).astype(jnp.bfloat16)
    ones = jnp.ones((8, 128), jnp.bfloat16)
    dims = (((1,), (1,)), ((), ()))
    total = lax.dot_general(ones, high, dims, preferred_element_type=jnp.float32) + lax.dot_general(
        ones, low, dims, preferred_element_type=jnp.float32
    )
    return (0.5 * ALPHA) * total[0:1, :]


def to_column(row):
    return jnp.transpose(jnp.broadcast_to(row, (128, 128)))


def kernel(
    xs, ys, am, bm, f_out, g_out,
    X, Y, ST, CB, amv, bmv, aux_t, aux_s, r_rows, part_f, recv_f, part_g, recv_g, f_part, f_all, part_e, recv_e,
    local_sem, x_recv, fwd_recv, y_recv, at_recv, as_recv, send_sem,
    f_send, f_recv, g_send, g_recv, o_send, o_recv, e_send, e_recv,
):
    s = lax.axis_index("src")
    t = lax.axis_index("tgt")
    z = (s // 4) * 4 + t // 8
    y = s % 4
    x = (t // 2) % 4
    c = t % 2
    zl = z % 4
    tile = y * 4 + x
    q = chunk_of(z)
    line = lambda p: place((z + p) % 8, y, x, c)

    copies = [
        pltpu.make_async_copy(ys, Y.at[q], local_sem.at[0]),
        pltpu.make_async_copy(xs, X.at[tile, pl.ds(c * 64, 64)], local_sem.at[1]),
        pltpu.make_async_copy(bm, bmv, local_sem.at[2]),
        pltpu.make_async_copy(am, amv, local_sem.at[3]),
    ]
    for copy in copies:
        copy.start()

    barrier = pltpu.get_barrier_semaphore()

    def greet_line(p, carry):
        pl.semaphore_signal(barrier, inc=1, device_id=line(p), device_id_type=MESH)
        return carry

    def greet_plane(p, carry):
        pl.semaphore_signal(barrier, inc=1, device_id=plane_peer(p, z, y, x, c), device_id_type=MESH)
        return carry

    def greet_rest(p, carry):
        pl.semaphore_signal(
            barrier, inc=1, device_id=place((z + 1 + p % 7) % 8, (y + 1 + p // 7) % 4, x, c), device_id_type=MESH
        )
        return carry

    lax.fori_loop(0, 21, greet_rest, 0)
    lax.fori_loop(1, 8, greet_line, 0)
    lax.fori_loop(1, 32, greet_plane, 0)

    for copy in copies:
        copy.wait()
    norm = row_norm(Y[q])
    aux_t[q, 0:1, :] = log2(bmv[pl.ds(s, 1), :]) - norm
    aux_t[q, 1:2, :] = norm
    aux_s[tile] = log2(amv[pl.ds(t // 2, 1), :])

    pl.semaphore_wait(barrier, 7 + 31 + 21)

    def remote(src, dst, send, recv, device):
        pltpu.make_async_remote_copy(
            src_ref=src, dst_ref=dst, send_sem=send, recv_sem=recv, device_id=device, device_id_type=MESH
        ).start()

    def send_aux_t(p, carry):
        remote(aux_t.at[q], aux_t.at[q], send_sem.at[0], at_recv.at[0], line(p))
        return carry

    def send_y(k, carry):
        p = (4 + (k // 2 + k % 2) * (1 - 2 * (k % 2))) % 8
        remote(Y.at[q], Y.at[q], send_sem.at[1], y_recv.at[q], line(p))
        return carry

    own = (tile, pl.ds(c * 64, 64))

    def send_x(p, carry):
        device = plane_peer(p * 2, z, y, x, c)
        remote(X.at[own], X.at[own], send_sem.at[2], x_recv.at[tile], device)
        return carry

    def send_aux_s(p, carry):
        device = plane_peer(p * 2, z, y, x, c)
        remote(aux_s.at[tile], aux_s.at[tile], send_sem.at[3], as_recv.at[0], device)
        return carry

    sibling = place(z, y, x, 1 - c)
    lax.fori_loop(1, 8, send_aux_t, 0)
    lax.fori_loop(0, 7, send_y, 0)
    lax.fori_loop(1, 16, send_x, 0)
    lax.fori_loop(1, 16, send_aux_s, 0)
    remote(X.at[own], X.at[own], send_sem.at[4], fwd_recv.at[0], sibling)

    def forward(p, carry):
        there = ((y + p // 4) % 4) * 4 + (x + p % 4) % 4
        block = (there, pl.ds(c * 64, 64))
        pltpu.make_async_copy(X.at[block], X.at[block], x_recv.at[there]).wait()
        remote(X.at[block], X.at[block], send_sem.at[4], fwd_recv.at[0], sibling)
        return carry

    lax.fori_loop(1, 16, forward, 0)
    pltpu.make_async_copy(aux_t.at[pl.ds(0, 7)], aux_t.at[pl.ds(0, 7)], at_recv.at[0]).wait()
    pltpu.make_async_copy(aux_s.at[pl.ds(0, 15)], aux_s.at[pl.ds(0, 15)], as_recv.at[0]).wait()

    def columns(k, carry):
        CB[k] = to_column(aux_t[k, 0:1, :])
        return carry

    lax.fori_loop(0, CHUNKS, columns, 0)
    others = (pl.ds(0, TILES), pl.ds((1 - c) * 64, 64))
    pltpu.make_async_copy(X.at[others], X.at[others], fwd_recv.at[0]).wait()

    def scores_chunk(k, carry):
        p = ((k + 1) // 2) * (2 * (k % 2) - 1) + 8
        there = chunk_of((z + p) % 8)

        @pl.when(k > 0)
        def _():
            pltpu.make_async_copy(Y.at[there], Y.at[there], y_recv.at[there]).wait()

        chosen = Y[there]

        def scores_tile(m, carry):
            for u in range(4):
                ST[there, m * 4 + u] = ALPHA * lax.dot_general(
                    chosen, X[m * 4 + u], (((1,), (1,)), ((), ())), preferred_element_type=jnp.float32
                )
            return carry

        lax.fori_loop(0, TILES // 4, scores_tile, 0)
        return carry

    lax.fori_loop(0, CHUNKS, scores_chunk, 0)

    def source_tile(m):
        peak = None
        for k in range(CHUNKS):
            block = (ST[k, m] + CB[k]).reshape(16, 8, 128)
            here = jnp.max(block, axis=0)
            total_here = jnp.sum(jnp.exp2(block - here[None]), axis=0)
            if peak is None:
                peak, total = here, total_here
            else:
                top = jnp.maximum(peak, here)
                total = total * jnp.exp2(peak - top) + total_here * jnp.exp2(here - top)
                peak = top
        top = jnp.max(peak, axis=0, keepdims=True)
        return top + log2(jnp.sum(total * jnp.exp2(peak - top), axis=0, keepdims=True))

    def target_chunk(k, parts):
        def block(j, carry):
            rows = pl.ds(j * 8, 8)
            pieces = [ST[k, m, rows, :] + r_rows[m // 8, m % 8 : m % 8 + 1, :] for m in range(TILES)]
            peak = pieces[0]
            for piece in pieces[1:]:
                peak = jnp.maximum(peak, piece)
            total = jnp.exp2(pieces[0] - peak)
            for piece in pieces[1:]:
                total = total + jnp.exp2(piece - peak)
            parts[rows, :] = peak + log2(total)
            return carry

        lax.fori_loop(0, 16, block, 0, unroll=2)
        turned = jnp.transpose(parts[...])
        top = jnp.max(turned, axis=0, keepdims=True)
        return top + log2(jnp.sum(jnp.exp2(turned - top), axis=0, keepdims=True))

    def merge(parts):
        top = jnp.max(parts, axis=0)
        return top + log2(jnp.sum(jnp.exp2(parts - top[None]), axis=0))

    for step in range(ITERS):
        last = step == ITERS - 1
        for half in range(HALVES):

            def one_tile(m, carry):
                part_f[step, half, pl.ds(m, 1), :] = source_tile(half * 8 + m)
                return carry

            lax.fori_loop(0, 8, one_tile, 0)

            def send_f(p, carry):
                remote(
                    part_f.at[step, half], recv_f.at[step, half, p - 1], f_send.at[step, half], f_recv.at[step, half],
                    plane_peer(p, z, y, x, c),
                )
                return carry

            lax.fori_loop(1, 32, send_f, 0)
        for half in range(HALVES):
            arrived = recv_f.at[step, half]
            pltpu.make_async_copy(arrived, arrived, f_recv.at[step, half]).wait()
            total = merge(jnp.concatenate([recv_f[step, half], part_f[step, half][None]], axis=0))
            r_rows[half] = jnp.concatenate([aux_s[half * 8 + m] for m in range(8)], axis=0) - total
            if last:
                for m in range(8):
                    there = half * 8 + m
                    f_part[there // 4, there % 4 : there % 4 + 1, :] = row_norm(X[there]) - total[m : m + 1, :]
        if last:
            f_all[zl] = f_part[y]
            for p in range(1, 4):
                device = place((z // 4) * 4 + (zl + p) % 4, y, x, c)
                remote(f_part.at[y], f_all.at[zl], o_send.at[0], o_recv.at[0], device)

        if not last:

            def one_chunk(k, carry):
                part_g[step, k // 2, pl.ds(k % 2, 1), :] = target_chunk(k, part_e)
                return carry

            lax.fori_loop(0, CHUNKS, one_chunk, 0)

            def send_g(p, carry):
                remote(part_g.at[step], recv_g.at[step, p - 1], g_send.at[step], g_recv.at[step], line(p))
                return carry

            lax.fori_loop(1, 8, send_g, 0)
            arrived = recv_g.at[step]
            pltpu.make_async_copy(arrived, arrived, g_recv.at[step]).wait()
            total = merge(jnp.concatenate([recv_g[step], part_g[step][None]], axis=0))
            part_g[2] = total

            def columns_next(k, carry):
                row = pl.ds(k % 2, 1)
                CB[k] = to_column(aux_t[k, 0:1, :] + aux_t[k, 1:2, :] - part_g[2, k // 2, row, :])
                return carry

            lax.fori_loop(0, CHUNKS, columns_next, 0)
        else:

            def last_chunk(k, carry):
                part_g[step, k // 2, pl.ds(k % 2, 1), :] = target_chunk(k, part_e) - aux_t[k, 1:2, :]
                return carry

            lax.fori_loop(0, CHUNKS, last_chunk, 0)

            def send_e(p, carry):
                there = (z + p % 8) % 8
                remote(
                    part_g.at[step, there % 4], recv_e.at[y * 8 + z], e_send.at[0], e_recv.at[0],
                    place(there, (y + p // 8) % 4, x, c),
                )
                return carry

            lax.fori_loop(1, 32, send_e, 0)
            recv_e[y * 8 + z] = part_g[step, zl]
            others = recv_e.at[pl.ds(0, 31)]
            pltpu.make_async_copy(others, others, e_recv.at[0]).wait()
            for there in range(4):
                total = merge(recv_e[there * 8 : there * 8 + 8])
                for half in range(2):
                    g_out[half * 4 + there : half * 4 + there + 1, :] = -total[half : half + 1, :]

    arrived = f_all.at[pl.ds(0, 3)]
    pltpu.make_async_copy(arrived, arrived, o_recv.at[0]).wait()
    for there in range(4):
        f_out[there * 4 : there * 4 + 4, :] = f_all[there]

    def sent(ref, sem):
        pltpu.make_async_copy(ref, ref, sem).wait()

    sent(aux_t.at[pl.ds(0, 7)], send_sem.at[0])
    sent(Y.at[pl.ds(0, 7)], send_sem.at[1])
    sent(X.at[pl.ds(0, 15), pl.ds(0, 64)], send_sem.at[2])
    sent(aux_s.at[pl.ds(0, 15)], send_sem.at[3])
    sent(X.at[pl.ds(0, 16), pl.ds(0, 64)], send_sem.at[4])
    for step in range(ITERS):
        for half in range(HALVES):
            sent(recv_f.at[step, half], f_send.at[step, half])
        if step < ITERS - 1:
            sent(recv_g.at[step], g_send.at[step])
    sent(f_all.at[pl.ds(0, 3)], o_send.at[0])
    sent(recv_e.at[pl.ds(0, 31)], e_send.at[0])


def local(source_points, target_points, source_mass, target_mass):
    f32, bf16 = jnp.float32, jnp.bfloat16
    dma = pltpu.SemaphoreType.DMA
    f_scaled, g_scaled = pl.pallas_call(
        kernel,
        out_shape=(jax.ShapeDtypeStruct((16, 128), f32), jax.ShapeDtypeStruct((8, 128), f32)),
        in_specs=[pl.BlockSpec(memory_space=pl.ANY)] * 4,
        out_specs=[pl.BlockSpec(memory_space=pltpu.VMEM)] * 2,
        scratch_shapes=[
            pltpu.VMEM((TILES, 128, 128), bf16),
            pltpu.VMEM((CHUNKS, 128, 128), bf16),
            pltpu.VMEM((CHUNKS, TILES, 128, 128), f32),
            pltpu.VMEM((CHUNKS, 128, 128), f32),
            pltpu.VMEM((16, 128), f32),
            pltpu.VMEM((8, 128), f32),
            pltpu.VMEM((CHUNKS, 2, 128), f32),
            pltpu.VMEM((TILES, 1, 128), f32),
            pltpu.VMEM((2, 8, 128), f32),
            pltpu.VMEM((ITERS, HALVES, 8, 128), f32),
            pltpu.VMEM((ITERS, HALVES, 31, 8, 128), f32),
            pltpu.VMEM((ITERS, 4, 2, 128), f32),
            pltpu.VMEM((ITERS - 1, 7, 4, 2, 128), f32),
            pltpu.VMEM((4, 4, 128), f32),
            pltpu.VMEM((4, 4, 128), f32),
            pltpu.VMEM((128, 128), f32),
            pltpu.VMEM((32, 2, 128), f32),
            dma((4,)),
            dma((TILES,)),
            dma((1,)),
            dma((CHUNKS,)),
            dma((1,)),
            dma((1,)),
            dma((5,)),
            dma((ITERS, HALVES)),
            dma((ITERS, HALVES)),
            dma((ITERS,)),
            dma((ITERS,)),
            dma((1,)),
            dma((1,)),
            dma((1,)),
            dma((1,)),
        ],
        compiler_params=pltpu.CompilerParams(collective_id=0, has_side_effects=True, vmem_limit_bytes=40 * 2**20),
    )(source_points, target_points, source_mass.reshape(16, 128), target_mass.reshape(8, 128))
    return f_scaled.reshape(2048) * (1.0 / ALPHA), g_scaled.reshape(1024) * (1.0 / ALPHA)


def solution(mesh):
    placed = (P(("src", "tgt"), None), P(("tgt", "src"), None), P("src"), P("tgt"))
    return jax.shard_map(
        local, mesh=mesh, in_specs=placed, out_specs=(P("src"), P("tgt")), check_vma=False
    )
```

time: 685 us -> 89.4 us (0.13); the launches traced: 678 us -> 89.1 us
  blocking collectives: 648 us -> 0 us
  Pallas kernels: 0 us -> 84.5 us
  matrix products: 13.5 us -> 0 us
  other arithmetic: 13 us -> 1.2 us
    pmax x6 -> x0, blocking collectives: 290 us -> none  [the longest x3 219 us: finish_rows(): widest = lax.pmax(peak, 'tgt')]
    psum x6 -> x0, blocking collectives: 266 us -> none  [the longest x3 206 us: finish_rows(): total = lax.psum(total * jnp.exp(peak - widest), 'tgt')]
    all_gather x2 -> x0, blocking collectives: 91.6 us -> none  [the longest x1 50.5 us: local(): sources = lax.all_gather(source_points, 'tgt', axis=0, tiled=True)]
    pallas_call x0 -> x1, Pallas kernels: none -> 84.5 us  [local(): pl.pallas_call(kernel, out_shape=(jax.ShapeDtypeStruct((16, 128), f32), j...]
    dot_general x24 -> x0, matrix products: 13.5 us -> none  [tile_cost(): jnp.dot(rows, cols.T, preferred_element_type=jnp.float32)]
    reduce_sum x26 -> x0, other arithmetic: 10.8 us -> none  [the longest x12 6.18 us: row_stats(): return (peak, jnp.sum(jnp.exp(scores - peak[:, None]), axis=1))]
where the time goes in v1:
time: 89.4 us; the launch traced here: 89.1 us
  Pallas kernels  84.5 us (95%)
  local copies, waits for them, and re-layouts  2.85 us (3%)
  other arithmetic  1.2 us (1%)
    pallas_call x1, Pallas kernels, local(): pl.pallas_call(kernel, out_shape=(jax.ShapeDtypeStruct((16, 128), f32), j...  84.5 us
    unnamed x8, local copies, waits for them, and re-layouts  2.85 us

profile of v1, /device:TPU:1, one launch (start us, length us, event | category | flops | bytes accessed | tf_op | source)
XLA Modules:
  0.0 89.1 jit_solution(11595758620348369008)
XLA Ops:
  0.6 0.0 copy-start
  0.6 0.7 copy-done
  1.4 0.0 copy-start.1
  1.4 0.7 copy-done.1
  2.1 0.0 copy-start.2
  2.1 0.7 copy-done.2
  2.8 0.0 copy-start.3
  2.8 0.7 copy-done.3
  3.5 84.5 %shard_map.59 = (f32[16,128]{1,0:T(8,128)S(1)}, f32[8,128]{1,0:T(8,128)S(1)}) custom-call(bf16[64,128]{1,0:T(8,128)(2,1)S(1)} %copy-done.1, bf16[128,128]{1,0:T(8,128)(2,1)S(1)} %copy-done, f32[16,128]{1,0:T(8,128)S(1)} %bitcast.6, f32[8,128]{1,0:T(8,128)S(1)} %bitcast.7), custom_call_target="tpu_custom_call" | custom-call | tf_op jit(solution)/shard_map/pallas_call | solution.py:328
  88.0 0.6 multiply_bitcast_fusion
  88.6 0.6 multiply_bitcast_fusion.1
Async XLA Ops:
  0.6 0.8 copy-start
  1.4 0.7 copy-start.1
  2.1 0.7 copy-start.2
  2.8 0.7 copy-start.3

commit v2 on v1

v2 whole, which is shorter than its diff:
```python
import math

import jax
import jax.numpy as jnp
from jax import lax
from jax.experimental import pallas as pl
from jax.experimental.pallas import tpu as pltpu
from jax.sharding import PartitionSpec as P

MESH = pl.DeviceIdType.MESH

ITERS = 3
EPS = 0.05
ALPHA = 1.0 / (EPS * math.log(2.0))
INV_LN2 = 1.0 / math.log(2.0)

TILES = 16
CHUNKS = 8
LOW = -1e30
VMEM_LIMIT = 60 * 2**20


def log2(value):
    return jnp.log(value) * INV_LN2


def place(z, y, x, c):
    return {"src": (z // 4) * 4 + y, "tgt": (z % 4) * 8 + x * 2 + c}


def chunk_of(z):
    return (z % 4) * 2 + z // 4


def plane_peer(p, z, y, x, c):
    return place(z, (y + p // 8) % 4, (x + (p // 2) % 4) % 4, (c + p % 2) % 2)


def near_first(k):
    return ((k + 1) // 2 * (2 * (k % 2) - 1) + 8) % 8


def row_norm(points):
    values = points.astype(jnp.float32)
    square = values * values
    high = square.astype(jnp.bfloat16)
    low = (square - high.astype(jnp.float32)).astype(jnp.bfloat16)
    ones = jnp.ones((8, 128), jnp.bfloat16)
    dims = (((1,), (1,)), ((), ()))
    total = lax.dot_general(ones, high, dims, preferred_element_type=jnp.float32) + lax.dot_general(
        ones, low, dims, preferred_element_type=jnp.float32
    )
    return (0.5 * ALPHA) * total[0:1, :]


def to_column(row):
    return jnp.transpose(jnp.broadcast_to(row, (128, 128)))


def tree(op, values):
    values = list(values)
    while len(values) > 1:
        values = [op(*values[i : i + 2]) if i + 1 < len(values) else values[i] for i in range(0, len(values), 2)]
    return values[0]


def stats(pieces):
    peak = tree(jnp.maximum, pieces)
    return peak, tree(jnp.add, [jnp.exp2(piece - peak) for piece in pieces])


def join(first, second):
    peak = jnp.maximum(first[0], second[0])
    return peak, first[1] * jnp.exp2(first[0] - peak) + second[1] * jnp.exp2(second[0] - peak)


def merge(parts, own):
    top = jnp.maximum(jnp.max(parts, axis=0), own)
    return top + log2(jnp.sum(jnp.exp2(parts - top[None]), axis=0) + jnp.exp2(own - top))


def kernel(
    xs, ys, am, bm, f_out, g_out,
    X, Y, ST, CB, GM, GT, PM, PT, amv, bmv, aux_t, aux_s, logs_a, norm_x, r_rows,
    part_f, recv_f, part_g, recv_g, f_part, f_all, part_e, recv_e,
    local_sem, x_recv, fwd_recv, y_recv, at_recv, as_recv, send_sem,
    f_send, f_recv, g_send, g_recv, o_send, o_recv, e_send, e_recv,
):
    s = lax.axis_index("src")
    t = lax.axis_index("tgt")
    z = (s // 4) * 4 + t // 8
    y = s % 4
    x = (t // 2) % 4
    c = t % 2
    zl = z % 4
    tile = y * 4 + x
    q = chunk_of(z)
    line = lambda p: place((z + p) % 8, y, x, c)

    copies = [
        pltpu.make_async_copy(ys, Y.at[q], local_sem.at[0]),
        pltpu.make_async_copy(xs, X.at[tile, pl.ds(c * 64, 64)], local_sem.at[1]),
        pltpu.make_async_copy(bm, bmv, local_sem.at[2]),
        pltpu.make_async_copy(am, amv, local_sem.at[3]),
    ]
    for copy in copies:
        copy.start()

    barrier = pltpu.get_barrier_semaphore()

    def greet_line(p, carry):
        pl.semaphore_signal(barrier, inc=1, device_id=line(p), device_id_type=MESH)
        return carry

    def greet_plane(p, carry):
        pl.semaphore_signal(barrier, inc=1, device_id=plane_peer(p, z, y, x, c), device_id_type=MESH)
        return carry

    lax.fori_loop(1, 8, greet_line, 0)
    lax.fori_loop(1, 32, greet_plane, 0)

    for copy in copies:
        copy.wait()
    norm = row_norm(Y[q])
    aux_t[q, 0:1, :] = log2(bmv[pl.ds(s, 1), :]) - norm
    aux_t[q, 1:2, :] = norm
    aux_s[tile] = log2(amv[pl.ds(t // 2, 1), :])
    GM[...] = jnp.full((TILES, 8, 128), LOW, jnp.float32)
    GT[...] = jnp.zeros((TILES, 8, 128), jnp.float32)

    pl.semaphore_wait(barrier, 7 + 31)

    def remote(src, dst, send, recv, device):
        pltpu.make_async_remote_copy(
            src_ref=src, dst_ref=dst, send_sem=send, recv_sem=recv, device_id=device, device_id_type=MESH
        ).start()

    def arrived(ref, sem):
        pltpu.make_async_copy(ref, ref, sem).wait()

    def send_aux_t(p, carry):
        remote(aux_t.at[q], aux_t.at[q], send_sem.at[0], at_recv.at[0], line(p))
        return carry

    def send_y(k, carry):
        remote(Y.at[q], Y.at[q], send_sem.at[1], y_recv.at[q], line(near_first(7 - k)))
        return carry

    own = (tile, pl.ds(c * 64, 64))

    def send_x(p, carry):
        remote(X.at[own], X.at[own], send_sem.at[2], x_recv.at[tile], plane_peer(p * 2, z, y, x, c))
        return carry

    def send_aux_s(p, carry):
        remote(aux_s.at[tile], aux_s.at[tile], send_sem.at[3], as_recv.at[0], plane_peer(p * 2, z, y, x, c))
        return carry

    sibling = place(z, y, x, 1 - c)
    lax.fori_loop(1, 8, send_aux_t, 0)
    lax.fori_loop(0, 7, send_y, 0)
    lax.fori_loop(1, 16, send_x, 0)
    remote(X.at[own], X.at[own], send_sem.at[4], fwd_recv.at[tile], sibling)
    lax.fori_loop(1, 16, send_aux_s, 0)

    arrived(aux_t.at[pl.ds(0, 7)], at_recv.at[0])
    for k in range(CHUNKS):
        CB[k] = to_column(aux_t[k, 0:1, :])

    def row_of(n):
        return (y + (n + 1) // 2 * (2 * (n % 2) - 1) + 4) % 4

    def forward(n):
        for x_there in range(4):
            there = row_of(n) * 4 + x_there
            block = (there, pl.ds(c * 64, 64))

            @pl.when(there != tile)
            def _():
                arrived(X.at[block], x_recv.at[there])
                remote(X.at[block], X.at[block], send_sem.at[4], fwd_recv.at[there], sibling)

    def send_f(step, half):
        def to_peer(p, carry):
            remote(
                part_f.at[step, half], recv_f.at[step, half, p - 1], f_send.at[step, half], f_recv.at[step, half],
                plane_peer(p, z, y, x, c),
            )
            return carry

        lax.fori_loop(1, 32, to_peer, 0)

    def finish_sources(step, half):
        peaks = GM[pl.ds(half * 8, 8)]
        top = jnp.max(peaks, axis=1)
        total = jnp.sum(GT[pl.ds(half * 8, 8)] * jnp.exp2(peaks - top[:, None, :]), axis=1)
        part_f[step, half] = top + log2(total)
        send_f(step, half)

    forward(0)

    def scores(i, carry):
        pair = i // 4
        n = i % 4
        later = (pair + 3) // 4
        group = (later * n + (1 - later) * row_of(n)) % 4

        @pl.when(pair == 0)
        def _():
            @pl.when(n < 3)
            def _():
                forward(n + 1)

            for x_there in range(4):
                there = group * 4 + x_there
                arrived(X.at[there, pl.ds((1 - c) * 64, 64)], fwd_recv.at[there])

        chunks = [chunk_of((z + near_first(pair * 2 + u)) % 8) for u in range(2)]

        @pl.when(n == 0)
        def _():
            @pl.when(pair > 0)
            def _():
                arrived(Y.at[chunks[0]], y_recv.at[chunks[0]])

            arrived(Y.at[chunks[1]], y_recv.at[chunks[1]])

        rows = jnp.concatenate([Y[k] for k in chunks], axis=0)
        tiles = X[pl.ds(group * 4, 4)].reshape(512, 128)
        product = lax.dot_general(rows, tiles, (((1,), (1,)), ((), ())), preferred_element_type=jnp.float32)
        for m in range(4):
            found = []
            for u in range(2):
                pieces = []
                for j in range(16):
                    piece = ALPHA * product[(u * 16 + j) * 8 : (u * 16 + j + 1) * 8, m * 128 : (m + 1) * 128]
                    ST[chunks[u], group * 4 + m, j * 8 : j * 8 + 8, :] = piece
                    pieces.append(piece + CB[chunks[u], j * 8 : j * 8 + 8, :])
                found.append(stats(pieces))
            GM[group * 4 + m], GT[group * 4 + m] = join((GM[group * 4 + m], GT[group * 4 + m]), join(*found))

        @pl.when((pair == 3) & (n % 2 == 1))
        def _():
            finish_sources(0, n // 2)

        return carry

    lax.fori_loop(0, 16, scores, 0)

    arrived(aux_s.at[pl.ds(0, 15)], as_recv.at[0])
    for half in range(2):
        logs_a[half] = jnp.concatenate([aux_s[half * 8 + m] for m in range(8)], axis=0)

    def norms(m, carry):
        norm_x[m] = row_norm(X[m])
        return carry

    lax.fori_loop(0, TILES, norms, 0)

    def merged_f(step, half):
        arrived(recv_f.at[step, half], f_recv.at[step, half])
        total = merge(recv_f[step, half], part_f[step, half])
        r_rows[half] = logs_a[half] - total
        return total

    def target_pieces(k, j, half):
        return [
            ST[k, half * 8 + m, j * 8 : j * 8 + 8, :] + r_rows[half, m : m + 1, :] for m in range(8)
        ]

    def target_first():
        def chunk(k, carry):
            for j in range(16):
                rows = slice(j * 8, j * 8 + 8)
                PM[k, rows, :], PT[k, rows, :] = stats(target_pieces(k, j, 0))
            return carry

        lax.fori_loop(0, CHUNKS, chunk, 0)

    def target_second(half):
        def chunk(i, carry):
            k = half * 4 + i
            for j in range(16):
                rows = slice(j * 8, j * 8 + 8)
                PM[k, rows, :], PT[k, rows, :] = join((PM[k, rows, :], PT[k, rows, :]), stats(target_pieces(k, j, 1)))
            return carry

        lax.fori_loop(0, 4, chunk, 0)
        results = []
        for i in range(4):
            peak, total = jnp.transpose(PM[half * 4 + i]), jnp.transpose(PT[half * 4 + i])
            top = jnp.max(peak, axis=0, keepdims=True)
            results.append(top + log2(jnp.sum(total * jnp.exp2(peak - top), axis=0, keepdims=True)))
        return results

    def merged_g(step, half):
        arrived(recv_g.at[step, half], g_recv.at[step, half])
        total = merge(recv_g[step, half], part_g[step, half])
        for i in range(4):
            k = half * 4 + i
            CB[k] = to_column(aux_t[k, 0:1, :] + aux_t[k, 1:2, :] - total[i : i + 1, :])

    def source_tiles(first, half):
        for u in range(4):
            m = first + u
            for k in range(half * 4, half * 4 + 4):
                found = stats(
                    [ST[k, m, j * 8 : j * 8 + 8, :] + CB[k, j * 8 : j * 8 + 8, :] for j in range(16)]
                )
                state = found if k == half * 4 else join(state, found)
            if half == 1:
                state = join((GM[m], GT[m]), state)
            GM[m], GT[m] = state

    def iteration(step, carry):
        merged_f(step, 0)
        target_first()
        merged_f(step, 1)

        def target_half(half, carry):
            for i, row in enumerate(target_second(half)):
                part_g[step, half, i : i + 1, :] = row

            def send_g(p, carry):
                remote(part_g.at[step, half], recv_g.at[step, half, p - 1], g_send.at[step, half], g_recv.at[step, half], line(p))
                return carry

            return lax.fori_loop(1, 8, send_g, carry)

        lax.fori_loop(0, 2, target_half, 0)

        merged_g(step, 0)

        def first_tiles(i, carry):
            source_tiles(i * 4, 0)
            return carry

        lax.fori_loop(0, 4, first_tiles, 0)
        merged_g(step, 1)

        def source_half(half, carry):
            def more_tiles(i, carry):
                source_tiles(half * 8 + i * 4, 1)
                return carry

            lax.fori_loop(0, 2, more_tiles, 0)
            finish_sources(step + 1, half)
            return carry

        return lax.fori_loop(0, 2, source_half, carry)

    lax.fori_loop(0, ITERS - 1, iteration, 0)

    last = ITERS - 1

    def put_f(half, total):
        for m in range(8):
            there = half * 8 + m
            f_part[there // 4, there % 4 : there % 4 + 1, :] = norm_x[there] - total[m : m + 1, :]

    put_f(0, merged_f(last, 0))
    target_first()
    put_f(1, merged_f(last, 1))
    f_all[zl] = f_part[y]
    for p in range(1, 4):
        device = place((z // 4) * 4 + (zl + p) % 4, y, x, c)
        remote(f_part.at[y], f_all.at[zl], o_send.at[0], o_recv.at[0], device)

    def last_half(half, carry):
        for i, row in enumerate(target_second(half)):
            part_e[half * 2 + i // 2, i % 2 : i % 2 + 1, :] = row - aux_t[half * 4 + i, 1:2, :]

        def send_e(i, carry):
            y_there = i // 4
            z_there = (i // 2) % 2 * 4 + half * 2 + i % 2

            @pl.when((y_there != y) | (z_there != z))
            def _():
                remote(
                    part_e.at[z_there % 4], recv_e.at[y * 8 + z], e_send.at[0], e_recv.at[0],
                    place(z_there, y_there, x, c),
                )

            return carry

        return lax.fori_loop(0, 16, send_e, carry)

    lax.fori_loop(0, 2, last_half, 0)
    recv_e[y * 8 + z] = part_e[zl]

    arrived(f_all.at[pl.ds(0, 3)], o_recv.at[0])
    for there in range(4):
        f_out[there * 4 : there * 4 + 4, :] = f_all[there]
    arrived(recv_e.at[pl.ds(0, 31)], e_recv.at[0])
    for there in range(4):
        parts = recv_e[there * 8 : there * 8 + 8]
        total = merge(parts[1:], parts[0])
        for half in range(2):
            g_out[half * 4 + there : half * 4 + there + 1, :] = -total[half : half + 1, :]

    arrived(aux_t.at[pl.ds(0, 7)], send_sem.at[0])
    arrived(Y.at[pl.ds(0, 7)], send_sem.at[1])
    arrived(X.at[pl.ds(0, 15), pl.ds(0, 64)], send_sem.at[2])
    arrived(aux_s.at[pl.ds(0, 15)], send_sem.at[3])
    arrived(X.at[pl.ds(0, 16), pl.ds(0, 64)], send_sem.at[4])
    for step in range(ITERS):
        for half in range(2):
            arrived(recv_f.at[step, half], f_send.at[step, half])
            if step < last:
                arrived(recv_g.at[step, half], g_send.at[step, half])
    arrived(f_all.at[pl.ds(0, 3)], o_send.at[0])
    arrived(recv_e.at[pl.ds(0, 31)], e_send.at[0])


def local(source_points, target_points, source_mass, target_mass):
    f32, bf16 = jnp.float32, jnp.bfloat16
    dma = pltpu.SemaphoreType.DMA
    f_scaled, g_scaled = pl.pallas_call(
        kernel,
        out_shape=(jax.ShapeDtypeStruct((16, 128), f32), jax.ShapeDtypeStruct((8, 128), f32)),
        in_specs=[pl.BlockSpec(memory_space=pl.ANY)] * 4,
        out_specs=[pl.BlockSpec(memory_space=pltpu.VMEM)] * 2,
        scratch_shapes=[
            pltpu.VMEM((TILES, 128, 128), bf16),
            pltpu.VMEM((CHUNKS, 128, 128), bf16),
            pltpu.VMEM((CHUNKS, TILES, 128, 128), f32),
            pltpu.VMEM((CHUNKS, 128, 128), f32),
            pltpu.VMEM((TILES, 8, 128), f32),
            pltpu.VMEM((TILES, 8, 128), f32),
            pltpu.VMEM((CHUNKS, 128, 128), f32),
            pltpu.VMEM((CHUNKS, 128, 128), f32),
            pltpu.VMEM((16, 128), f32),
            pltpu.VMEM((8, 128), f32),
            pltpu.VMEM((CHUNKS, 2, 128), f32),
            pltpu.VMEM((TILES, 1, 128), f32),
            pltpu.VMEM((2, 8, 128), f32),
            pltpu.VMEM((TILES, 1, 128), f32),
            pltpu.VMEM((2, 8, 128), f32),
            pltpu.VMEM((ITERS, 2, 8, 128), f32),
            pltpu.VMEM((ITERS, 2, 31, 8, 128), f32),
            pltpu.VMEM((ITERS - 1, 2, 4, 128), f32),
            pltpu.VMEM((ITERS - 1, 2, 7, 4, 128), f32),
            pltpu.VMEM((4, 4, 128), f32),
            pltpu.VMEM((4, 4, 128), f32),
            pltpu.VMEM((4, 2, 128), f32),
            pltpu.VMEM((32, 2, 128), f32),
            dma((4,)),
            dma((TILES,)),
            dma((TILES,)),
            dma((CHUNKS,)),
            dma((1,)),
            dma((1,)),
            dma((5,)),
            dma((ITERS, 2)),
            dma((ITERS, 2)),
            dma((ITERS - 1, 2)),
            dma((ITERS - 1, 2)),
            dma((1,)),
            dma((1,)),
            dma((1,)),
            dma((1,)),
        ],
        compiler_params=pltpu.CompilerParams(collective_id=0, has_side_effects=True, vmem_limit_bytes=VMEM_LIMIT),
    )(source_points, target_points, source_mass.reshape(16, 128), target_mass.reshape(8, 128))
    return f_scaled.reshape(2048) * (1.0 / ALPHA), g_scaled.reshape(1024) * (1.0 / ALPHA)


def solution(mesh):
    placed = (P(("src", "tgt"), None), P(("tgt", "src"), None), P("src"), P("tgt"))
    return jax.shard_map(
        local, mesh=mesh, in_specs=placed, out_specs=(P("src"), P("tgt")), check_vma=False
    )
```

time: 89.4 us -> 70.1 us (0.78)
  Pallas kernels: 84.5 us -> 67.4 us
  local copies, waits for them, and re-layouts: 2.85 us -> 0.01 us
    pallas_call x1, Pallas kernels: 84.5 us -> 67.4 us  [local(): pl.pallas_call(kernel, out_shape=(jax.ShapeDtypeStruct((16, 128), f32), j...]
    unnamed x8 -> x2, local copies, waits for them, and re-layouts: 2.85 us -> 0.01 us
where the time goes in v2:
time: 70.1 us; the launch traced here: 69.9 us
  Pallas kernels  67.4 us (96%)
  other arithmetic  1.89 us (3%)
    pallas_call x1, Pallas kernels, local(): pl.pallas_call(kernel, out_shape=(jax.ShapeDtypeStruct((16, 128), f32), j...  67.4 us

profile of v2, /device:TPU:1, one launch (start us, length us, event | category | flops | bytes accessed | tf_op | source)
XLA Modules:
  0.0 69.9 jit_solution(3463804608622424781)
XLA Ops:
  0.6 67.4 %shard_map.59 = (f32[16,128]{1,0:T(8,128)}, f32[8,128]{1,0:T(8,128)}) custom-call(bf16[64,128]{1,0:T(8,128)(2,1)} %xs.1, bf16[128,128]{1,0:T(8,128)(2,1)} %ys.1, f32[16,128]{1,0:T(8,128)} %bitcast.6, f32[8,128]{1,0:T(8,128)} %bitcast.7), custom_call_target="tpu_custom_call" | custom-call | tf_op jit(solution)/shard_map/pallas_call | solution.py:418
  68.0 0.0 copy-start
  68.0 1.3 %multiply_bitcast_fusion = f32[2048]{0:T(1024)} fusion(f32[16,128]{1,0:T(8,128)} %get-tuple-element.4), kind=kLoop, calls=%fused_computation | loop fusion | flops 2048 | bytes 16384 | tf_op jit(solution)/shard_map/mul | solution.py:465
  69.3 0.0 copy-done
  69.3 0.6 multiply_bitcast_fusion.1
Async XLA Ops:
  68.0 1.3 %copy-start = (f32[8,128]{1,0:T(8,128)S(1)}, f32[8,128]{1,0:T(8,128)}, u32[]{:S(2)}) copy-start(f32[8,128]{1,0:T(8,128)} %get-tuple-element.5) | copy-start | bytes 12292

commit v3 on v2

--- a/solution.py
+++ b/solution.py
@@ -16,8 +16,15 @@
 
 TILES = 16
 CHUNKS = 8
-LOW = -1e30
-VMEM_LIMIT = 60 * 2**20
+LINE = (4, 3, 5, 2, 6, 1, 7)
+ORDER = (1, 7, 2, 6, 3, 5, 4)
+SETS = ((0, 1, 7, 2), (6, 3, 5, 4))
+PLANE = sorted(
+    ((dy, dx, dc) for dy in range(4) for dx in range(4) for dc in range(2) if dy or dx or dc),
+    key=lambda p: -min(p[0], 4 - p[0]) - min(p[1], 4 - p[1]),
+)
+CHIPS = [p for p in PLANE if p[2] == 0]
+VMEM_LIMIT = 24 * 2**20
 
 
 def log2(value):
@@ -30,14 +37,6 @@
 
 def chunk_of(z):
     return (z % 4) * 2 + z // 4
-
-
-def plane_peer(p, z, y, x, c):
-    return place(z, (y + p // 8) % 4, (x + (p // 2) % 4) % 4, (c + p % 2) % 2)
-
-
-def near_first(k):
-    return ((k + 1) // 2 * (2 * (k % 2) - 1) + 8) % 8
 
 
 def row_norm(points):
@@ -95,7 +94,24 @@
     zl = z % 4
     tile = y * 4 + x
     q = chunk_of(z)
-    line = lambda p: place((z + p) % 8, y, x, c)
+
+    z_at = [(z + p) % 8 for p in range(8)]
+    src_z = [there // 4 * 4 for there in z_at]
+    tgt_z = [there % 4 * 8 for there in z_at]
+    y_at = [(y + p) % 4 for p in range(4)]
+    tgt_x = [(x + p) % 4 * 2 for p in range(4)]
+    tgt_c = [c, 1 - c]
+    tgt_xc = [[tgt_z[0] + tgt_x[p] + tgt_c[r] for r in range(2)] for p in range(4)]
+    src_y = [src_z[0] + y_at[p] for p in range(4)]
+    tgt_own = tgt_x[0] + c
+
+    def line(p):
+        return {"src": src_z[p] + y, "tgt": tgt_z[p] + tgt_own}
+
+    def plane(p):
+        return {"src": src_y[p[0]], "tgt": tgt_xc[p[1]][p[2]]}
+
+    sibling = plane((0, 0, 1))
 
     copies = [
         pltpu.make_async_copy(ys, Y.at[q], local_sem.at[0]),
@@ -108,16 +124,10 @@
 
     barrier = pltpu.get_barrier_semaphore()
 
-    def greet_line(p, carry):
+    for p in LINE:
         pl.semaphore_signal(barrier, inc=1, device_id=line(p), device_id_type=MESH)
-        return carry
-
-    def greet_plane(p, carry):
-        pl.semaphore_signal(barrier, inc=1, device_id=plane_peer(p, z, y, x, c), device_id_type=MESH)
-        return carry
-
-    lax.fori_loop(1, 8, greet_line, 0)
-    lax.fori_loop(1, 32, greet_plane, 0)
+    for p in PLANE:
+        pl.semaphore_signal(barrier, inc=1, device_id=plane(p), device_id_type=MESH)
 
     for copy in copies:
         copy.wait()
@@ -125,8 +135,6 @@
     aux_t[q, 0:1, :] = log2(bmv[pl.ds(s, 1), :]) - norm
     aux_t[q, 1:2, :] = norm
     aux_s[tile] = log2(amv[pl.ds(t // 2, 1), :])
-    GM[...] = jnp.full((TILES, 8, 128), LOW, jnp.float32)
-    GT[...] = jnp.zeros((TILES, 8, 128), jnp.float32)
 
     pl.semaphore_wait(barrier, 7 + 31)
 
@@ -138,34 +146,16 @@
     def arrived(ref, sem):
         pltpu.make_async_copy(ref, ref, sem).wait()
 
-    def send_aux_t(p, carry):
+    own = (tile, pl.ds(c * 64, 64))
+    for p in LINE:
         remote(aux_t.at[q], aux_t.at[q], send_sem.at[0], at_recv.at[0], line(p))
-        return carry
-
-    def send_y(k, carry):
-        remote(Y.at[q], Y.at[q], send_sem.at[1], y_recv.at[q], line(near_first(7 - k)))
-        return carry
-
-    own = (tile, pl.ds(c * 64, 64))
-
-    def send_x(p, carry):
-        remote(X.at[own], X.at[own], send_sem.at[2], x_recv.at[tile], plane_peer(p * 2, z, y, x, c))
-        return carry
-
-    def send_aux_s(p, carry):
-        remote(aux_s.at[tile], aux_s.at[tile], send_sem.at[3], as_recv.at[0], plane_peer(p * 2, z, y, x, c))
-        return carry
-
-    sibling = place(z, y, x, 1 - c)
-    lax.fori_loop(1, 8, send_aux_t, 0)
-    lax.fori_loop(0, 7, send_y, 0)
-    lax.fori_loop(1, 16, send_x, 0)
+    for p in ORDER:
+        remote(Y.at[q], Y.at[q], send_sem.at[1], y_recv.at[q], line(p))
+    for p in CHIPS:
+        remote(X.at[own], X.at[own], send_sem.at[2], x_recv.at[tile], plane(p))
     remote(X.at[own], X.at[own], send_sem.at[4], fwd_recv.at[tile], sibling)
-    lax.fori_loop(1, 16, send_aux_s, 0)
-
-    arrived(aux_t.at[pl.ds(0, 7)], at_recv.at[0])
-    for k in range(CHUNKS):
-        CB[k] = to_column(aux_t[k, 0:1, :])
+    for p in CHIPS:
+        remote(aux_s.at[tile], aux_s.at[tile], send_sem.at[3], as_recv.at[0], plane(p))
 
     def row_of(n):
         return (y + (n + 1) // 2 * (2 * (n % 2) - 1) + 4) % 4
@@ -181,14 +171,10 @@
                 remote(X.at[block], X.at[block], send_sem.at[4], fwd_recv.at[there], sibling)
 
     def send_f(step, half):
-        def to_peer(p, carry):
+        for i, p in enumerate(PLANE):
             remote(
-                part_f.at[step, half], recv_f.at[step, half, p - 1], f_send.at[step, half], f_recv.at[step, half],
-                plane_peer(p, z, y, x, c),
+                part_f.at[step, half], recv_f.at[step, half, i], f_send.at[step, half], f_recv.at[step, half], plane(p)
             )
-            return carry
-
-        lax.fori_loop(1, 32, to_peer, 0)
 
     def finish_sources(step, half):
         peaks = GM[pl.ds(half * 8, 8)]
@@ -197,55 +183,56 @@
         part_f[step, half] = top + log2(total)
         send_f(step, half)
 
-    forward(0)
-
-    def scores(i, carry):
-        pair = i // 4
-        n = i % 4
-        later = (pair + 3) // 4
-        group = (later * n + (1 - later) * row_of(n)) % 4
-
-        @pl.when(pair == 0)
-        def _():
-            @pl.when(n < 3)
-            def _():
-                forward(n + 1)
-
-            for x_there in range(4):
-                there = group * 4 + x_there
-                arrived(X.at[there, pl.ds((1 - c) * 64, 64)], fwd_recv.at[there])
-
-        chunks = [chunk_of((z + near_first(pair * 2 + u)) % 8) for u in range(2)]
-
-        @pl.when(n == 0)
-        def _():
-            @pl.when(pair > 0)
-            def _():
-                arrived(Y.at[chunks[0]], y_recv.at[chunks[0]])
-
-            arrived(Y.at[chunks[1]], y_recv.at[chunks[1]])
-
+    def scores(first, count, chunks, add):
         rows = jnp.concatenate([Y[k] for k in chunks], axis=0)
-        tiles = X[pl.ds(group * 4, 4)].reshape(512, 128)
+        tiles = X[pl.ds(first, count)].reshape(count * 128, 128)
         product = lax.dot_general(rows, tiles, (((1,), (1,)), ((), ())), preferred_element_type=jnp.float32)
-        for m in range(4):
+        for m in range(count):
             found = []
-            for u in range(2):
+            for u, k in enumerate(chunks):
                 pieces = []
                 for j in range(16):
                     piece = ALPHA * product[(u * 16 + j) * 8 : (u * 16 + j + 1) * 8, m * 128 : (m + 1) * 128]
-                    ST[chunks[u], group * 4 + m, j * 8 : j * 8 + 8, :] = piece
-                    pieces.append(piece + CB[chunks[u], j * 8 : j * 8 + 8, :])
+                    ST[k, first + m, j * 8 : j * 8 + 8, :] = piece
+                    pieces.append(piece + CB[k, j * 8 : j * 8 + 8, :])
                 found.append(stats(pieces))
-            GM[group * 4 + m], GT[group * 4 + m] = join((GM[group * 4 + m], GT[group * 4 + m]), join(*found))
-
-        @pl.when((pair == 3) & (n % 2 == 1))
+            if add:
+                found.append((GM[first + m], GT[first + m]))
+            GM[first + m], GT[first + m] = tree(join, found)
+
+    def chunks_at(distances):
+        return [chunk_of(z_at[p]) for p in distances]
+
+    for n in range(3):
+        forward(n)
+    arrived(aux_t.at[pl.ds(0, 7)], at_recv.at[0])
+    for k in range(CHUNKS):
+        CB[k] = to_column(aux_t[k, 0:1, :])
+    for k in chunks_at(SETS[0])[1:]:
+        arrived(Y.at[k], y_recv.at[k])
+
+    def early(n, carry):
+        @pl.when(n == 1)
         def _():
-            finish_sources(0, n // 2)
-
+            forward(3)
+
+        row = row_of(n)
+        for x_there in range(4):
+            there = row * 4 + x_there
+            arrived(X.at[there, pl.ds((1 - c) * 64, 64)], fwd_recv.at[there])
+        scores(row * 4, 4, chunks_at(SETS[0]), False)
         return carry
 
-    lax.fori_loop(0, 16, scores, 0)
+    lax.fori_loop(0, 4, early, 0)
+    for k in chunks_at(SETS[1]):
+        arrived(Y.at[k], y_recv.at[k])
+
+    def late(half, carry):
+        scores(half * 8, 8, chunks_at(SETS[1]), True)
+        finish_sources(0, half)
+        return carry
+
+    lax.fori_loop(0, 2, late, 0)
 
     arrived(aux_s.at[pl.ds(0, 15)], as_recv.at[0])
     for half in range(2):
@@ -321,11 +308,11 @@
             for i, row in enumerate(target_second(half)):
                 part_g[step, half, i : i + 1, :] = row
 
-            def send_g(p, carry):
-                remote(part_g.at[step, half], recv_g.at[step, half, p - 1], g_send.at[step, half], g_recv.at[step, half], line(p))
-                return carry
-
-            return lax.fori_loop(1, 8, send_g, carry)
+            for i, p in enumerate(LINE):
+                remote(
+                    part_g.at[step, half], recv_g.at[step, half, i], g_send.at[step, half], g_recv.at[step, half], line(p)
+                )
+            return carry
 
         lax.fori_loop(0, 2, target_half, 0)
 
@@ -461,7 +448,7 @@
             dma((1,)),
         ],
         compiler_params=pltpu.CompilerParams(collective_id=0, has_side_effects=True, vmem_limit_bytes=VMEM_LIMIT),
-    )(source_points, target_points, source_mass.reshape(16, 128), target_mass.reshape(8, 128))
+    )(*[pltpu.with_memory_space_constraint(v, pltpu.HBM) for v in (source_points, target_points, source_mass.reshape(16, 128), target_mass.reshape(8, 128))])
     return f_scaled.reshape(2048) * (1.0 / ALPHA), g_scaled.reshape(1024) * (1.0 / ALPHA)
 
 

time: 70.1 us -> 61 us (0.87)
  Pallas kernels: 67.4 us -> 59.1 us
    pallas_call x1, Pallas kernels: 67.4 us -> 59.1 us  [local(): pl.pallas_call(kernel, out_shape=(jax.ShapeDtypeStruct((16, 128), f32), j...]
where the time goes in v3:
time: 61 us; the launch traced here: 60.9 us
  Pallas kernels  59.1 us (97%)
  other arithmetic  1.2 us (2%)
  between operations  0.64 us (1%)
    pallas_call x1, Pallas kernels, local(): pl.pallas_call(kernel, out_shape=(jax.ShapeDtypeStruct((16, 128), f32), j...  59.1 us

profile of v3, /device:TPU:1, one launch (start us, length us, event | category | flops | bytes accessed | tf_op | source)
XLA Modules:
  0.0 60.9 jit_solution(3605887918895706829)
XLA Ops:
  0.6 59.1 %shard_map.59 = (f32[16,128]{1,0:T(8,128)S(1)}, f32[8,128]{1,0:T(8,128)S(1)}) custom-call(bf16[64,128]{1,0:T(8,128)(2,1)} %xs.1, bf16[128,128]{1,0:T(8,128)(2,1)} %ys.1, f32[16,128]{1,0:T(8,128)} %bitcast.6, f32[8,128]{1,0:T(8,128)} %bitcast.7), custom_call_target="tpu_custom_call" | custom-call | tf_op jit(solution)/shard_map/pallas_call | solution.py:405
  59.7 0.6 multiply_bitcast_fusion
  60.3 0.6 multiply_bitcast_fusion.1

commit v4 on v3

--- a/solution.py
+++ b/solution.py
@@ -17,13 +17,18 @@
 TILES = 16
 CHUNKS = 8
 LINE = (4, 3, 5, 2, 6, 1, 7)
-ORDER = (1, 7, 2, 6, 3, 5, 4)
-SETS = ((0, 1, 7, 2), (6, 3, 5, 4))
+ORDER = (2, 6, 3, 5, 1, 7)
+SETS = ((0, 1, 7, 2, 6), (3, 5, 4))
 PLANE = sorted(
     ((dy, dx, dc) for dy in range(4) for dx in range(4) for dc in range(2) if dy or dx or dc),
     key=lambda p: -min(p[0], 4 - p[0]) - min(p[1], 4 - p[1]),
 )
+SHEET = sorted(
+    ((dy, dz) for dy in range(4) for dz in range(8) if dy or dz), key=lambda p: -min(p[0], 4 - p[0]) - min(p[1], 8 - p[1])
+)
 CHIPS = [p for p in PLANE if p[2] == 0]
+FAR = 9
+FAR_CHIPS = [p for p in CHIPS if min(p[0], 4 - p[0]) + min(p[1], 4 - p[1]) >= FAR]
 VMEM_LIMIT = 24 * 2**20
 
 
@@ -98,7 +103,9 @@
     z_at = [(z + p) % 8 for p in range(8)]
     src_z = [there // 4 * 4 for there in z_at]
     tgt_z = [there % 4 * 8 for there in z_at]
+    zl_at = [there % 4 for there in z_at]
     y_at = [(y + p) % 4 for p in range(4)]
+    x_at = [(x + p) % 4 for p in range(4)]
     tgt_x = [(x + p) % 4 * 2 for p in range(4)]
     tgt_c = [c, 1 - c]
     tgt_xc = [[tgt_z[0] + tgt_x[p] + tgt_c[r] for r in range(2)] for p in range(4)]
@@ -153,6 +160,8 @@
         remote(Y.at[q], Y.at[q], send_sem.at[1], y_recv.at[q], line(p))
     for p in CHIPS:
         remote(X.at[own], X.at[own], send_sem.at[2], x_recv.at[tile], plane(p))
+    for dy, dx, _ in FAR_CHIPS:
+        remote(X.at[own], X.at[own], send_sem.at[4], fwd_recv.at[tile], plane((dy, dx, 1)))
     remote(X.at[own], X.at[own], send_sem.at[4], fwd_recv.at[tile], sibling)
     for p in CHIPS:
         remote(aux_s.at[tile], aux_s.at[tile], send_sem.at[3], as_recv.at[0], plane(p))
@@ -161,12 +170,11 @@
         return (y + (n + 1) // 2 * (2 * (n % 2) - 1) + 4) % 4
 
     def forward(n):
-        for x_there in range(4):
-            there = row_of(n) * 4 + x_there
-            block = (there, pl.ds(c * 64, 64))
-
-            @pl.when(there != tile)
-            def _():
+        dy = (0, 1, 3, 2)[n]
+        for dx in (0, 1, 3, 2):
+            if (dy, dx) != (0, 0) and (dy, dx, 0) not in FAR_CHIPS:
+                there = y_at[dy] * 4 + x_at[dx]
+                block = (there, pl.ds(c * 64, 64))
                 arrived(X.at[block], x_recv.at[there])
                 remote(X.at[block], X.at[block], send_sem.at[4], fwd_recv.at[there], sibling)
 
@@ -205,26 +213,37 @@
 
     for n in range(3):
         forward(n)
+        if n == 0:
+            for p, rows in ((2, pl.ds(0, 64)), (6, pl.ds(64, 64))):
+                k = chunk_of(z_at[p])
+                arrived(Y.at[k], y_recv.at[k])
+                remote(Y.at[k, rows], Y.at[k, rows], send_sem.at[5], y_recv.at[k], line(8 - p))
     arrived(aux_t.at[pl.ds(0, 7)], at_recv.at[0])
     for k in range(CHUNKS):
         CB[k] = to_column(aux_t[k, 0:1, :])
-    for k in chunks_at(SETS[0])[1:]:
+    forward(3)
+    for k in chunks_at(p for p in SETS[0] if p not in (0, 2, 6)):
         arrived(Y.at[k], y_recv.at[k])
 
+    def hops(n, x_there):
+        dx = (x_there - x + 4) % 4
+        return (n + 1) // 2 + dx - dx // 3 * 2
+
     def early(n, carry):
-        @pl.when(n == 1)
-        def _():
-            forward(3)
-
         row = row_of(n)
         for x_there in range(4):
             there = row * 4 + x_there
             arrived(X.at[there, pl.ds((1 - c) * 64, 64)], fwd_recv.at[there])
+
+            @pl.when(hops(n, x_there) >= FAR)
+            def _():
+                arrived(X.at[there, pl.ds(c * 64, 64)], x_recv.at[there])
+
         scores(row * 4, 4, chunks_at(SETS[0]), False)
         return carry
 
     lax.fori_loop(0, 4, early, 0)
-    for k in chunks_at(SETS[1]):
+    for k in chunks_at(p for p in SETS[1] if p not in (0, 2, 6)):
         arrived(Y.at[k], y_recv.at[k])
 
     def late(half, carry):
@@ -299,80 +318,80 @@
                 state = join((GM[m], GT[m]), state)
             GM[m], GT[m] = state
 
+    last = ITERS - 1
+
     def iteration(step, carry):
-        merged_f(step, 0)
+        first = merged_f(step, 0)
         target_first()
-        merged_f(step, 1)
+        second = merged_f(step, 1)
 
         def target_half(half, carry):
-            for i, row in enumerate(target_second(half)):
-                part_g[step, half, i : i + 1, :] = row
-
-            for i, p in enumerate(LINE):
-                remote(
-                    part_g.at[step, half], recv_g.at[step, half, i], g_send.at[step, half], g_recv.at[step, half], line(p)
-                )
+            rows = target_second(half)
+
+            @pl.when(step < last)
+            def _():
+                for i, row in enumerate(rows):
+                    part_g[step, half, i : i + 1, :] = row
+                for i, p in enumerate(LINE):
+                    remote(
+                        part_g.at[step, half], recv_g.at[step, half, i], g_send.at[step, half], g_recv.at[step, half], line(p)
+                    )
+
+            @pl.when(step == last)
+            def _():
+                for i, row in enumerate(rows):
+                    part_e[half * 2 + i // 2, i % 2 : i % 2 + 1, :] = row - aux_t[half * 4 + i, 1:2, :]
+                for dy, dz in SHEET:
+
+                    @pl.when(zl_at[dz] // 2 == half)
+                    def _():
+                        remote(
+                            part_e.at[zl_at[dz]], recv_e.at[y * 8 + z], e_send.at[0], e_recv.at[0],
+                            {"src": src_z[dz] + y_at[dy], "tgt": tgt_z[dz] + tgt_own},
+                        )
+
+
             return carry
 
         lax.fori_loop(0, 2, target_half, 0)
 
-        merged_g(step, 0)
-
-        def first_tiles(i, carry):
-            source_tiles(i * 4, 0)
-            return carry
-
-        lax.fori_loop(0, 4, first_tiles, 0)
-        merged_g(step, 1)
-
-        def source_half(half, carry):
-            def more_tiles(i, carry):
-                source_tiles(half * 8 + i * 4, 1)
+        @pl.when(step < last)
+        def _():
+            merged_g(step, 0)
+
+            def first_tiles(i, carry):
+                source_tiles(i * 4, 0)
                 return carry
 
-            lax.fori_loop(0, 2, more_tiles, 0)
-            finish_sources(step + 1, half)
-            return carry
-
-        return lax.fori_loop(0, 2, source_half, carry)
-
-    lax.fori_loop(0, ITERS - 1, iteration, 0)
-
-    last = ITERS - 1
-
-    def put_f(half, total):
-        for m in range(8):
-            there = half * 8 + m
-            f_part[there // 4, there % 4 : there % 4 + 1, :] = norm_x[there] - total[m : m + 1, :]
-
-    put_f(0, merged_f(last, 0))
-    target_first()
-    put_f(1, merged_f(last, 1))
+            lax.fori_loop(0, 4, first_tiles, 0)
+            merged_g(step, 1)
+
+            def source_half(half, carry):
+                def more_tiles(i, carry):
+                    source_tiles(half * 8 + i * 4, 1)
+                    return carry
+
+                lax.fori_loop(0, 2, more_tiles, 0)
+                finish_sources(step + 1, half)
+                return carry
+
+            lax.fori_loop(0, 2, source_half, 0)
+
+        @pl.when(step == last)
+        def _():
+            for half, total in enumerate((first, second)):
+                for m in range(8):
+                    there = half * 8 + m
+                    f_part[there // 4, there % 4 : there % 4 + 1, :] = norm_x[there] - total[m : m + 1, :]
+
+        return carry
+
+    lax.fori_loop(0, ITERS, iteration, 0)
+
     f_all[zl] = f_part[y]
     for p in range(1, 4):
-        device = place((z // 4) * 4 + (zl + p) % 4, y, x, c)
+        device = {"src": src_y[0], "tgt": (zl + p) % 4 * 8 + tgt_own}
         remote(f_part.at[y], f_all.at[zl], o_send.at[0], o_recv.at[0], device)
-
-    def last_half(half, carry):
-        for i, row in enumerate(target_second(half)):
-            part_e[half * 2 + i // 2, i % 2 : i % 2 + 1, :] = row - aux_t[half * 4 + i, 1:2, :]
-
-        def send_e(i, carry):
-            y_there = i // 4
-            z_there = (i // 2) % 2 * 4 + half * 2 + i % 2
-
-            @pl.when((y_there != y) | (z_there != z))
-            def _():
-                remote(
-                    part_e.at[z_there % 4], recv_e.at[y * 8 + z], e_send.at[0], e_recv.at[0],
-                    place(z_there, y_there, x, c),
-                )
-
-            return carry
-
-        return lax.fori_loop(0, 16, send_e, carry)
-
-    lax.fori_loop(0, 2, last_half, 0)
     recv_e[y * 8 + z] = part_e[zl]
 
     arrived(f_all.at[pl.ds(0, 3)], o_recv.at[0])
@@ -386,7 +405,8 @@
             g_out[half * 4 + there : half * 4 + there + 1, :] = -total[half : half + 1, :]
 
     arrived(aux_t.at[pl.ds(0, 7)], send_sem.at[0])
-    arrived(Y.at[pl.ds(0, 7)], send_sem.at[1])
+    arrived(Y.at[pl.ds(0, 6)], send_sem.at[1])
+    arrived(Y.at[0], send_sem.at[5])
     arrived(X.at[pl.ds(0, 15), pl.ds(0, 64)], send_sem.at[2])
     arrived(aux_s.at[pl.ds(0, 15)], send_sem.at[3])
     arrived(X.at[pl.ds(0, 16), pl.ds(0, 64)], send_sem.at[4])
@@ -437,7 +457,7 @@
             dma((CHUNKS,)),
             dma((1,)),
             dma((1,)),
-            dma((5,)),
+            dma((6,)),
             dma((ITERS, 2)),
             dma((ITERS, 2)),
             dma((ITERS - 1, 2)),

time: 61 us -> 60.6 us (level)
  no operation moved by 1% of the time
where the time goes in v4:
time: 60.6 us; the launch traced here: 60.4 us
  Pallas kernels  58.6 us (97%)
  other arithmetic  1.2 us (2%)
  between operations  0.64 us (1%)
    pallas_call x1, Pallas kernels, local(): pl.pallas_call(kernel, out_shape=(jax.ShapeDtypeStruct((16, 128), f32), j...  58.6 us

profile of v4, /device:TPU:1, one launch (start us, length us, event | category | flops | bytes accessed | tf_op | source)
XLA Modules:
  0.0 60.4 jit_solution(5164579617699279991)
XLA Ops:
  0.6 58.6 %shard_map.59 = (f32[16,128]{1,0:T(8,128)S(1)}, f32[8,128]{1,0:T(8,128)S(1)}) custom-call(bf16[64,128]{1,0:T(8,128)(2,1)} %xs.1, bf16[128,128]{1,0:T(8,128)(2,1)} %ys.1, f32[16,128]{1,0:T(8,128)} %bitcast.6, f32[8,128]{1,0:T(8,128)} %bitcast.7), custom_call_target="tpu_custom_call" | custom-call | tf_op jit(solution)/shard_map/pallas_call | solution.py:425
  59.2 0.6 multiply_bitcast_fusion
  59.8 0.6 multiply_bitcast_fusion.1

commit v5 on v4

--- a/solution.py
+++ b/solution.py
@@ -275,28 +275,27 @@
         ]
 
     def target_first():
-        def chunk(k, carry):
+        def chunk(i, carry):
+            for k in (i * 2, i * 2 + 1):
+                for j in range(16):
+                    rows = slice(j * 8, j * 8 + 8)
+                    PM[k, rows, :], PT[k, rows, :] = stats(target_pieces(k, j, 0))
+            return carry
+
+        lax.fori_loop(0, CHUNKS // 2, chunk, 0)
+
+    def target_second(half):
+        results = []
+        for i in range(4):
+            k = half * 4 + i
+            values = []
             for j in range(16):
                 rows = slice(j * 8, j * 8 + 8)
-                PM[k, rows, :], PT[k, rows, :] = stats(target_pieces(k, j, 0))
-            return carry
-
-        lax.fori_loop(0, CHUNKS, chunk, 0)
-
-    def target_second(half):
-        def chunk(i, carry):
-            k = half * 4 + i
-            for j in range(16):
-                rows = slice(j * 8, j * 8 + 8)
-                PM[k, rows, :], PT[k, rows, :] = join((PM[k, rows, :], PT[k, rows, :]), stats(target_pieces(k, j, 1)))
-            return carry
-
-        lax.fori_loop(0, 4, chunk, 0)
-        results = []
-        for i in range(4):
-            peak, total = jnp.transpose(PM[half * 4 + i]), jnp.transpose(PT[half * 4 + i])
-            top = jnp.max(peak, axis=0, keepdims=True)
-            results.append(top + log2(jnp.sum(total * jnp.exp2(peak - top), axis=0, keepdims=True)))
+                found = join((PM[k, rows, :], PT[k, rows, :]), stats(target_pieces(k, j, 1)))
+                values.append(found[0] + log2(found[1]))
+            turned = jnp.transpose(jnp.concatenate(values, axis=0))
+            top = jnp.max(turned, axis=0, keepdims=True)
+            results.append(top + log2(jnp.sum(jnp.exp2(turned - top), axis=0, keepdims=True)))
         return results
 
     def merged_g(step, half):
@@ -367,11 +366,8 @@
             merged_g(step, 1)
 
             def source_half(half, carry):
-                def more_tiles(i, carry):
+                for i in range(2):
                     source_tiles(half * 8 + i * 4, 1)
-                    return carry
-
-                lax.fori_loop(0, 2, more_tiles, 0)
                 finish_sources(step + 1, half)
                 return carry
 
@@ -397,13 +393,6 @@
     arrived(f_all.at[pl.ds(0, 3)], o_recv.at[0])
     for there in range(4):
         f_out[there * 4 : there * 4 + 4, :] = f_all[there]
-    arrived(recv_e.at[pl.ds(0, 31)], e_recv.at[0])
-    for there in range(4):
-        parts = recv_e[there * 8 : there * 8 + 8]
-        total = merge(parts[1:], parts[0])
-        for half in range(2):
-            g_out[half * 4 + there : half * 4 + there + 1, :] = -total[half : half + 1, :]
-
     arrived(aux_t.at[pl.ds(0, 7)], send_sem.at[0])
     arrived(Y.at[pl.ds(0, 6)], send_sem.at[1])
     arrived(Y.at[0], send_sem.at[5])
@@ -417,6 +406,13 @@
                 arrived(recv_g.at[step, half], g_send.at[step, half])
     arrived(f_all.at[pl.ds(0, 3)], o_send.at[0])
     arrived(recv_e.at[pl.ds(0, 31)], e_send.at[0])
+
+    arrived(recv_e.at[pl.ds(0, 31)], e_recv.at[0])
+    for there in range(4):
+        parts = recv_e[there * 8 : there * 8 + 8]
+        total = merge(parts[1:], parts[0])
+        for half in range(2):
+            g_out[half * 4 + there : half * 4 + there + 1, :] = -total[half : half + 1, :]
 
 
 def local(source_points, target_points, source_mass, target_mass):

time: 60.6 us -> 59.9 us (0.988)
  Pallas kernels: 58.6 us -> 57.9 us
    pallas_call x1, Pallas kernels: 58.6 us -> 57.9 us  [local(): pl.pallas_call(kernel, out_shape=(jax.ShapeDtypeStruct((16, 128), f32), j...]
where the time goes in v5:
time: 59.9 us; the launch traced here: 59.8 us
  Pallas kernels  57.9 us (97%)
  other arithmetic  1.2 us (2%)
  between operations  0.64 us (1%)
    pallas_call x1, Pallas kernels, local(): pl.pallas_call(kernel, out_shape=(jax.ShapeDtypeStruct((16, 128), f32), j...  57.9 us

profile of v5, /device:TPU:1, one launch (start us, length us, event | category | flops | bytes accessed | tf_op | source)
XLA Modules:
  0.0 59.8 jit_solution(15777948994544229475)
XLA Ops:
  0.6 57.9 %shard_map.59 = (f32[16,128]{1,0:T(8,128)S(1)}, f32[8,128]{1,0:T(8,128)S(1)}) custom-call(bf16[64,128]{1,0:T(8,128)(2,1)} %xs.1, bf16[128,128]{1,0:T(8,128)(2,1)} %ys.1, f32[16,128]{1,0:T(8,128)} %bitcast.6, f32[8,128]{1,0:T(8,128)} %bitcast.7), custom_call_target="tpu_custom_call" | custom-call | tf_op jit(solution)/shard_map/pallas_call | solution.py:421
  58.6 0.6 %multiply_bitcast_fusion = f32[2048]{0:T(1024)} fusion(f32[16,128]{1,0:T(8,128)S(1)} %get-tuple-element.4), kind=kLoop, calls=%fused_computation | loop fusion | flops 2048 | bytes 16384 | tf_op jit(solution)/shard_map/mul | solution.py:468
  59.2 0.6 multiply_bitcast_fusion.1

commit v6 on v5

--- a/solution.py
+++ b/solution.py
@@ -27,8 +27,6 @@
     ((dy, dz) for dy in range(4) for dz in range(8) if dy or dz), key=lambda p: -min(p[0], 4 - p[0]) - min(p[1], 8 - p[1])
 )
 CHIPS = [p for p in PLANE if p[2] == 0]
-FAR = 9
-FAR_CHIPS = [p for p in CHIPS if min(p[0], 4 - p[0]) + min(p[1], 4 - p[1]) >= FAR]
 VMEM_LIMIT = 24 * 2**20
 
 
@@ -84,7 +82,7 @@
 
 
 def kernel(
-    xs, ys, am, bm, f_out, g_out,
+    xs, ys, am, bm, out,
     X, Y, ST, CB, GM, GT, PM, PT, amv, bmv, aux_t, aux_s, logs_a, norm_x, r_rows,
     part_f, recv_f, part_g, recv_g, f_part, f_all, part_e, recv_e,
     local_sem, x_recv, fwd_recv, y_recv, at_recv, as_recv, send_sem,
@@ -160,8 +158,6 @@
         remote(Y.at[q], Y.at[q], send_sem.at[1], y_recv.at[q], line(p))
     for p in CHIPS:
         remote(X.at[own], X.at[own], send_sem.at[2], x_recv.at[tile], plane(p))
-    for dy, dx, _ in FAR_CHIPS:
-        remote(X.at[own], X.at[own], send_sem.at[4], fwd_recv.at[tile], plane((dy, dx, 1)))
     remote(X.at[own], X.at[own], send_sem.at[4], fwd_recv.at[tile], sibling)
     for p in CHIPS:
         remote(aux_s.at[tile], aux_s.at[tile], send_sem.at[3], as_recv.at[0], plane(p))
@@ -172,7 +168,7 @@
     def forward(n):
         dy = (0, 1, 3, 2)[n]
         for dx in (0, 1, 3, 2):
-            if (dy, dx) != (0, 0) and (dy, dx, 0) not in FAR_CHIPS:
+            if (dy, dx) != (0, 0):
                 there = y_at[dy] * 4 + x_at[dx]
                 block = (there, pl.ds(c * 64, 64))
                 arrived(X.at[block], x_recv.at[there])
@@ -225,20 +221,11 @@
     for k in chunks_at(p for p in SETS[0] if p not in (0, 2, 6)):
         arrived(Y.at[k], y_recv.at[k])
 
-    def hops(n, x_there):
-        dx = (x_there - x + 4) % 4
-        return (n + 1) // 2 + dx - dx // 3 * 2
-
     def early(n, carry):
         row = row_of(n)
         for x_there in range(4):
             there = row * 4 + x_there
             arrived(X.at[there, pl.ds((1 - c) * 64, 64)], fwd_recv.at[there])
-
-            @pl.when(hops(n, x_there) >= FAR)
-            def _():
-                arrived(X.at[there, pl.ds(c * 64, 64)], x_recv.at[there])
-
         scores(row * 4, 4, chunks_at(SETS[0]), False)
         return carry
 
@@ -392,7 +379,7 @@
 
     arrived(f_all.at[pl.ds(0, 3)], o_recv.at[0])
     for there in range(4):
-        f_out[there * 4 : there * 4 + 4, :] = f_all[there]
+        out[there * 4 : there * 4 + 4, :] = f_all[there]
     arrived(aux_t.at[pl.ds(0, 7)], send_sem.at[0])
     arrived(Y.at[pl.ds(0, 6)], send_sem.at[1])
     arrived(Y.at[0], send_sem.at[5])
@@ -412,17 +399,17 @@
         parts = recv_e[there * 8 : there * 8 + 8]
         total = merge(parts[1:], parts[0])
         for half in range(2):
-            g_out[half * 4 + there : half * 4 + there + 1, :] = -total[half : half + 1, :]
+            out[16 + half * 4 + there : 17 + half * 4 + there, :] = -total[half : half + 1, :]
 
 
 def local(source_points, target_points, source_mass, target_mass):
     f32, bf16 = jnp.float32, jnp.bfloat16
     dma = pltpu.SemaphoreType.DMA
-    f_scaled, g_scaled = pl.pallas_call(
+    scaled = pl.pallas_call(
         kernel,
-        out_shape=(jax.ShapeDtypeStruct((16, 128), f32), jax.ShapeDtypeStruct((8, 128), f32)),
+        out_shape=jax.ShapeDtypeStruct((24, 128), f32),
         in_specs=[pl.BlockSpec(memory_space=pl.ANY)] * 4,
-        out_specs=[pl.BlockSpec(memory_space=pltpu.VMEM)] * 2,
+        out_specs=pl.BlockSpec(memory_space=pltpu.VMEM),
         scratch_shapes=[
             pltpu.VMEM((TILES, 128, 128), bf16),
             pltpu.VMEM((CHUNKS, 128, 128), bf16),
@@ -465,7 +452,7 @@
         ],
         compiler_params=pltpu.CompilerParams(collective_id=0, has_side_effects=True, vmem_limit_bytes=VMEM_LIMIT),
     )(*[pltpu.with_memory_space_constraint(v, pltpu.HBM) for v in (source_points, target_points, source_mass.reshape(16, 128), target_mass.reshape(8, 128))])
-    return f_scaled.reshape(2048) * (1.0 / ALPHA), g_scaled.reshape(1024) * (1.0 / ALPHA)
+    return scaled[:16].reshape(2048) * (1.0 / ALPHA), scaled[16:].reshape(1024) * (1.0 / ALPHA)
 
 
 def solution(mesh):

time: 59.9 us -> 59.7 us (level)
  no operation moved by 1% of the time
where the time goes in v6:
time: 59.7 us; the launch traced here: 59.6 us
  Pallas kernels  57.8 us (97%)
  other arithmetic  1.2 us (2%)
  between operations  0.64 us (1%)
    pallas_call x1, Pallas kernels, local(): pl.pallas_call(kernel, out_shape=jax.ShapeDtypeStruct((24, 128), f32), in...  57.8 us

profile of v6, /device:TPU:1, one launch (start us, length us, event | category | flops | bytes accessed | tf_op | source)
XLA Modules:
  0.0 59.6 jit_solution(11246062150947959740)
XLA Ops:
  0.6 57.8 %shard_map.59 = f32[24,128]{1,0:T(8,128)S(1)} custom-call(bf16[64,128]{1,0:T(8,128)(2,1)} %xs.1, bf16[128,128]{1,0:T(8,128)(2,1)} %ys.1, f32[16,128]{1,0:T(8,128)} %bitcast.6, f32[8,128]{1,0:T(8,128)} %bitcast.7), custom_call_target="tpu_custom_call" | custom-call | tf_op jit(solution)/shard_map/pallas_call | solution.py:408
  58.4 0.6 multiply_bitcast_fusion.1
  59.0 0.6 %multiply_bitcast_fusion = f32[2048]{0:T(1024)} fusion(f32[24,128]{1,0:T(8,128)S(1)} %shard_map.59), kind=kLoop, calls=%fused_computation | loop fusion | flops 2048 | bytes 16384 | tf_op jit(solution)/shard_map/mul | solution.py:455

commit v7 on v6

--- a/solution.py
+++ b/solution.py
@@ -17,7 +17,7 @@
 TILES = 16
 CHUNKS = 8
 LINE = (4, 3, 5, 2, 6, 1, 7)
-ORDER = (2, 6, 3, 5, 1, 7)
+ORDER = (2, 6, 1, 7)
 SETS = ((0, 1, 7, 2, 6), (3, 5, 4))
 PLANE = sorted(
     ((dy, dx, dc) for dy in range(4) for dx in range(4) for dc in range(2) if dy or dx or dc),
@@ -207,13 +207,13 @@
     def chunks_at(distances):
         return [chunk_of(z_at[p]) for p in distances]
 
+    for p, rows in ((2, pl.ds(0, 64)), (6, pl.ds(64, 64))):
+        k = chunk_of(z_at[p])
+        arrived(Y.at[k], y_recv.at[k])
+        remote(Y.at[k], Y.at[k], send_sem.at[5], y_recv.at[k], line(7 if p == 2 else 1))
+        remote(Y.at[k, rows], Y.at[k, rows], send_sem.at[5], y_recv.at[k], line(8 - p))
     for n in range(3):
         forward(n)
-        if n == 0:
-            for p, rows in ((2, pl.ds(0, 64)), (6, pl.ds(64, 64))):
-                k = chunk_of(z_at[p])
-                arrived(Y.at[k], y_recv.at[k])
-                remote(Y.at[k, rows], Y.at[k, rows], send_sem.at[5], y_recv.at[k], line(8 - p))
     arrived(aux_t.at[pl.ds(0, 7)], at_recv.at[0])
     for k in range(CHUNKS):
         CB[k] = to_column(aux_t[k, 0:1, :])
@@ -381,8 +381,8 @@
     for there in range(4):
         out[there * 4 : there * 4 + 4, :] = f_all[there]
     arrived(aux_t.at[pl.ds(0, 7)], send_sem.at[0])
-    arrived(Y.at[pl.ds(0, 6)], send_sem.at[1])
-    arrived(Y.at[0], send_sem.at[5])
+    arrived(Y.at[pl.ds(0, 4)], send_sem.at[1])
+    arrived(Y.at[pl.ds(0, 3)], send_sem.at[5])
     arrived(X.at[pl.ds(0, 15), pl.ds(0, 64)], send_sem.at[2])
     arrived(aux_s.at[pl.ds(0, 15)], send_sem.at[3])
     arrived(X.at[pl.ds(0, 16), pl.ds(0, 64)], send_sem.at[4])

time: 59.7 us -> 59.8 us (level)
  no operation moved by 1% of the time
where the time goes in v7:
time: 59.8 us; the launch traced here: 59.6 us
  Pallas kernels  57.8 us (97%)
  other arithmetic  1.2 us (2%)
  between operations  0.64 us (1%)
    pallas_call x1, Pallas kernels, local(): pl.pallas_call(kernel, out_shape=jax.ShapeDtypeStruct((24, 128), f32), in...  57.8 us

profile of v7, /device:TPU:1, one launch (start us, length us, event | category | flops | bytes accessed | tf_op | source)
XLA Modules:
  0.0 59.6 jit_solution(4626938424002243337)
XLA Ops:
  0.6 57.8 %shard_map.59 = f32[24,128]{1,0:T(8,128)S(1)} custom-call(bf16[64,128]{1,0:T(8,128)(2,1)} %xs.1, bf16[128,128]{1,0:T(8,128)(2,1)} %ys.1, f32[16,128]{1,0:T(8,128)} %bitcast.6, f32[8,128]{1,0:T(8,128)} %bitcast.7), custom_call_target="tpu_custom_call" | custom-call | tf_op jit(solution)/shard_map/pallas_call | solution.py:408
  58.4 0.6 multiply_bitcast_fusion.1
  59.0 0.6 %multiply_bitcast_fusion = f32[2048]{0:T(1024)} fusion(f32[24,128]{1,0:T(8,128)S(1)} %shard_map.59), kind=kLoop, calls=%fused_computation | loop fusion | flops 2048 | bytes 16384 | tf_op jit(solution)/shard_map/mul | solution.py:455
